TPU v7x, 32 devices: a whole 2x2x4 slice. The times are simulated.
32 devices in a mesh: parts: 2 (over y), owner: 8 (over z, core), rep: 2 (over x), sub: 1.
Axes of the slice: x: 2, y: 2, z: 4, core: 2. Of those that a mesh axis runs over, the one named last changes fastest.
Arguments:
- entity_rows: float32 [16384, 256], P(('parts', 'owner', 'rep', 'sub')), parts along dimension 0, may hold values from -1.5 to 1.5
- adagrad_sum: float32 [16384], P(('parts', 'owner', 'rep', 'sub')), parts along dimension 0, may hold values from 0.01 to 1
- src_local: int32 [16384], P(('parts', 'owner', 'rep', 'sub')), parts along dimension 0, may hold values from 0 to 511
- dst_part: int32 [16384, 1], P(('parts', 'owner', 'rep', 'sub')), parts along dimension 0, may hold values from 0 to 7; in each aligned block of 512 rows (0 to 511, 512 to 1023, ...) at most 96 rows name the same one
- dst_local: int32 [16384], P(('parts', 'owner', 'rep', 'sub')), parts along dimension 0, may hold values from 0 to 511
- rel_ids: int32 [16384], P(('parts', 'owner', 'rep', 'sub')), parts along dimension 0, may hold values from 0 to 1279
- neg_local: int32 [16384], P(('parts', 'owner', 'rep', 'sub')), parts along dimension 0, may hold values from 0 to 511
- edge_count: int32 [32], P(('parts', 'owner', 'rep', 'sub')), parts along dimension 0, may hold values from 32 to 512, as said below
- relations: float32 [1280, 256], replicated, may hold values from 0.1 to 1.9
Outputs:
- rows_new: float32 [16384, 256], P(('parts', 'owner', 'rep', 'sub')), parts along dimension 0
- adagrad_new: float32 [16384], P(('parts', 'owner', 'rep', 'sub')), parts along dimension 0
- relation_grad: float32 [2560, 256], P(('parts', 'owner', 'rep', 'sub')), parts along dimension 0
There are 2 independent parts, one for each index of `parts`. A program takes and returns all parts, laid end to end along the dimension named above; an argument that names none is the same for every part. Nothing has to cross between parts.
Inputs may be any that keep to these rules, and one draw needn't show every extreme that they name: `dst_part`: among the edges of one task no partition is named more than 96 times; in some tasks one partition is named exactly 96 times. `edge_count`: some task has all 512 edges active and some task only 32.
All inputs are finite; a program needn't handle non-finite values.
Results may differ from a plain program's by a relative error of at most 0.0003.
Values sent between devices are 32-bit elements; how exact they have to be, the bound alone decides.
A program may use at most 64 MiB of HBM per device.

v0:
```python
import jax
import jax.numpy as jnp
from jax import lax
from jax.sharding import PartitionSpec as P

step_size = 0.1


def body(
    entity_rows,
    adagrad_sum,
    src_local,
    dst_part,
    dst_local,
    rel_ids,
    neg_local,
    edge_count,
    relations,
):
    owners = lax.axis_size("owner")
    edge_total = src_local.shape[0]
    width = entity_rows.shape[1]
    slot_cap = edge_total // owners * 3 // 2
    dst_owner = dst_part[:, 0]
    one_hot = (dst_owner[:, None] == jnp.arange(owners, dtype=jnp.int32)[None, :]).astype(jnp.int32)
    before = jnp.cumsum(one_hot, axis=0) - one_hot
    slot_of = dst_owner * slot_cap + jnp.sum(before * one_hot, axis=1)
    wanted = jnp.zeros((owners * slot_cap,), jnp.int32).at[slot_of].set(dst_local)
    asked_ids = lax.all_to_all(wanted, "owner", split_axis=0, concat_axis=0, tiled=True)
    served = jnp.take(entity_rows, asked_ids, axis=0)
    fetched = lax.all_to_all(served, "owner", split_axis=0, concat_axis=0, tiled=True)
    source = jnp.take(entity_rows, src_local, axis=0)
    negatives = jnp.take(entity_rows, neg_local, axis=0)
    operator = jnp.take(relations, rel_ids, axis=0)
    queries = source * operator
    neg_scores = jnp.dot(
        queries, negatives.T, precision=lax.Precision.HIGHEST, preferred_element_type=jnp.float32
    )
    active = (jnp.arange(edge_total, dtype=jnp.int32) < edge_count[0]).astype(jnp.float32)
    neg_total = negatives.shape[0]
    grad_neg = jax.nn.sigmoid(neg_scores) * (active / neg_total)[:, None]
    grad_negative = jnp.dot(
        grad_neg.T, queries, precision=lax.Precision.HIGHEST, preferred_element_type=jnp.float32
    )
    neg_part = jnp.dot(
        grad_neg, negatives, precision=lax.Precision.HIGHEST, preferred_element_type=jnp.float32
    )
    target = jnp.take(fetched, slot_of, axis=0)
    positive = jnp.sum(queries * target, axis=1)
    grad_pos = -jax.nn.sigmoid(-positive) * active
    grad_target = grad_pos[:, None] * queries
    grad_query = grad_pos[:, None] * target + neg_part
    grad_source = grad_query * operator
    grad_operator = grad_query * source
    outgoing = jnp.zeros((owners * slot_cap, width), jnp.float32).at[slot_of].set(grad_target)
    rel_part = jnp.zeros(relations.shape, jnp.float32).at[rel_ids].add(grad_operator)
    incoming = lax.all_to_all(outgoing, "owner", split_axis=0, concat_axis=0, tiled=True)
    relation_grad = lax.psum_scatter(
        rel_part, ("owner", "rep", "sub"), scatter_dimension=0, tiled=True
    )
    grad_rows = jnp.zeros(entity_rows.shape, jnp.float32)
    grad_rows = (
        grad_rows.at[src_local]
        .add(grad_source)
        .at[neg_local]
        .add(grad_negative)
        .at[asked_ids]
        .add(incoming)
    )
    adagrad_new = adagrad_sum + jnp.mean(grad_rows * grad_rows, axis=1)
    rows_new = entity_rows - step_size * grad_rows / jnp.sqrt(adagrad_new)[:, None]
    return (rows_new, adagrad_new, relation_grad)


def solution(mesh):
    in_specs = (
        P(("parts", "owner", "rep", "sub"), None),
        P(("parts", "owner", "rep", "sub")),
        P(("parts", "owner", "rep", "sub")),
        P(("parts", "owner", "rep", "sub"), None),
        P(("parts", "owner", "rep", "sub")),
        P(("parts", "owner", "rep", "sub")),
        P(("parts", "owner", "rep", "sub")),
        P(("parts", "owner", "rep", "sub")),
        P(),
    )
    out_specs = (
        P(("parts", "owner", "rep", "sub"), None),
        P(("parts", "owner", "rep", "sub")),
        P(("parts", "owner", "rep", "sub"), None),
    )
    return jax.shard_map(body, mesh=mesh, in_specs=in_specs, out_specs=out_specs, check_vma=False)
```

profile of v0, /device:TPU:0, one launch (start us, length us, event | category | flops | bytes accessed | tf_op | source)
XLA Modules:
  0.0 144.4 jit_solution(2218038221251055261)
XLA Ops:
  7.2 0.8 fusion.28
  8.0 1.1 reduce-window.6
  9.4 0.8 fusion.27
  10.1 0.7 and_reduce_fusion
  10.8 2.6 %scatter_custom_fusion = s32[768]{0:T(1024)S(1)} fusion(s32[512]{0:T(512)S(1)} %bitcast.31, s32[512]{0:T(512)} %param.15, s32[]{:T(128)} %constant.43.clone.1), kind=kCustom, calls=%fused_computation.67 | custom fusion | bytes 3584 | tf_op jit(solution)/shard_map/scatter | solution.py:28
  13.4 0.7 all_to_all.24
  14.1 6.3 %all-to-all-start = ((s32[8,96,1]{1,2,0:T(1,128)}), s32[8,96,1]{1,2,0:T(1,128)S(1)}, u32[]{:S(2)}, u32[]{:S(2)}) async-start(s32[8,96,1]{1,2,0:T(1,128)} %all_to_all.24), calls=%async_computation | async-start | bytes 8192 | tf_op jit(solution)/shard_map/all_to_all | solution.py:29
  20.4 0.7 compare_select_fusion.5
  21.1 4.8 %all-to-all-done = s32[8,96,1]{1,2,0:T(1,128)S(1)} async-done(((s32[8,96,1]{1,2,0:T(1,128)}), s32[8,96,1]{1,2,0:T(1,128)S(1)}, u32[]{:S(2)}, u32[]{:S(2)}) %all-to-all-start) | async-done | bytes 3104 | tf_op jit(solution)/shard_map/all_to_all | solution.py:29
  26.4 0.7 reduce.9
  27.2 3.1 %gather_fusion.1 = f32[768,256]{1,0:T(8,128)S(1)} fusion(f32[512,256]{1,0:T(8,128)} %param.11, s32[1024]{0:T(1024)S(1)} %pad_clamp_fusion.2), kind=kCustom, calls=%fused_computation.3 | custom fusion | bytes 1575936 | tf_op jit(solution)/shard_map/jit(_take)/gather | solution.py:30
  30.4 1.0 broadcast_select_fusion
  31.5 3.5 %all-to-all-start.1 = ((f32[8,96,256]{2,1,0:T(8,128)}), f32[8,96,256]{2,1,0:T(8,128)S(1)}, u32[]{:S(2)}, u32[]{:S(2)}) async-start(f32[8,96,256]{2,1,0:T(8,128)} %broadcast_select_fusion), calls=%async_computation.1 | async-start | bytes 1572864 | tf_op jit(solution)/shard_map/all_to_all | solution.py:31
  35.0 2.3 %gather_fusion.3 = f32[512,256]{1,0:T(8,128)} fusion(f32[512,256]{1,0:T(8,128)S(1)} %copy-done.1, s32[1024]{0:T(1024)S(1)} %pad_clamp_fusion.4), kind=kCustom, calls=%fused_computation.clone | custom fusion | bytes 1050624 | tf_op jit(solution)/shard_map/jit(_take)/gather | solution.py:32
  37.3 2.2 %gather_fusion.4 = f32[512,256]{1,0:T(8,128)} fusion(f32[512,256]{1,0:T(8,128)S(1)} %copy-done.1, s32[1024]{0:T(1024)S(1)} %pad_clamp_fusion), kind=kCustom, calls=%fused_computation.1.clone | custom fusion | bytes 1050624 | tf_op jit(solution)/shard_map/jit(_take)/gather | solution.py:33
  40.3 1.6 %gather_fusion = f32[512,256]{1,0:T(8,128)S(1)} fusion(f32[1280,256]{1,0:T(8,128)S(1)} %copy-done, s32[1024]{0:T(1024)S(1)} %pad_clamp_fusion.3), kind=kCustom, calls=%fused_computation.2 | custom fusion | bytes 1050624 | tf_op jit(solution)/shard_map/jit(_take)/gather | solution.py:34
  41.9 14.0 %all-to-all-done.1 = f32[8,96,256]{2,1,0:T(8,128)S(1)} async-done(((f32[8,96,256]{2,1,0:T(8,128)}), f32[8,96,256]{2,1,0:T(8,128)S(1)}, u32[]{:S(2)}, u32[]{:S(2)}) %all-to-all-start.1) | async-done | bytes 786464 | tf_op jit(solution)/shard_map/all_to_all | solution.py:31
  55.9 2.2 %gather_fusion.2 = f32[512,256]{1,0:T(8,128)} fusion(f32[768,256]{1,0:T(8,128)S(1)} %bitcast.25, s32[1024]{0:T(1024)S(1)} %pad_clamp_fusion.1), kind=kCustom, calls=%fused_computation.4 | custom fusion | bytes 1050624 | tf_op jit(solution)/shard_map/jit(_take)/gather | solution.py:48
  58.1 1.6 %multiply_reduce_fusion.1 = (f32[512]{0:T(512)S(1)}, f32[512,256]{1,0:T(8,128)S(1)}) fusion(f32[512,256]{1,0:T(8,128)} %gather_fusion.2, pred[512]{0:T(512)(128)(4,1)S(1)} %get-tuple-element.8, f32[512,256]{1,0:T(8,128)S(1)} %gather_fusion, pred[512]{0:T(512)(128)(4,1)S(1)} %get-tuple-element.11, f32[512,256]{1,0:T(8,128)} %gather_fusion.3, ...), kind=kLoop, calls=%fused_computation.26 | loop fusion | flops 785920 | bytes 2100736 | tf_op jit(solution)/shard_map/reduce_sum | solution.py:49
  59.7 3.3 %scatter_custom_fusion.3 = f32[768,256]{1,0:T(8,128)} fusion(s32[512]{0:T(512)S(1)} %bitcast.33, f32[512,256]{1,0:T(8,128)S(1)} %get-tuple-element.7, f32[]{:T(128)} %constant.36.clone.1, f32[512]{0:T(512)S(1)} %negate_select_fusion), kind=kCustom, calls=%fused_computation.22 | custom fusion | flops 131072 | bytes 1312772 | tf_op jit(solution)/shard_map/scatter | solution.py:55
  63.0 4.2 %all-to-all-start.2 = ((f32[8,96,256]{2,1,0:T(8,128)}), f32[8,96,256]{2,1,0:T(8,128)}, u32[]{:S(2)}, u32[]{:S(2)}) async-start(f32[8,96,256]{2,1,0:T(8,128)} %bitcast.26), calls=%async_computation.2 | async-start | bytes 1572864 | tf_op jit(solution)/shard_map/all_to_all | solution.py:57
  67.5 2.4 %fusion.3 = f32[512,512]{1,0:T(8,128)S(1)} fusion(f32[512,256]{1,0:T(8,128)S(1)} %get-tuple-element.7, f32[512]{0:T(512)S(1)} %fusion.32, f32[512,256]{1,0:T(8,128)} %gather_fusion.4, pred[512]{0:T(512)(128)(4,1)S(1)} %compare_and_fusion.1), kind=kOutput, calls=%fused_computation.15 | convolution fusion | flops 806486016 | bytes 2099712 | tf_op jit(solution)/shard_map/dot_general | solution.py:36
  69.9 1.0 copy-done.6
  70.9 1.9 %convolution_add_fusion = f32[512,256]{1,0:T(8,128)} fusion(f32[512,512]{1,0:T(8,128)S(1)} %fusion.3, f32[512,256]{1,0:T(8,128)S(1)} %copy-done.7, f32[512,256]{1,0:T(8,128)S(1)} %copy-done.3, f32[512]{0:T(512)S(1)} %negate_select_fusion, pred[512]{0:T(512)(128)(4,1)S(1)} %compare_and_fusion.1, pred[512]{0:T(512)(128)(4,1)S(1)} %get-tuple-element.8), kind=kOutput, calls=%fused_computation.16 | convolution fusion | flops 805830656 | bytes 2624512 | tf_op jit(solution)/shard_map/dot_general | solution.py:45
  72.7 5.0 %scatter_custom_fusion.5 = f32[1280,256]{1,0:T(8,128)} fusion(s32[512]{0:T(512)S(1)} %compare_select_fusion.4, f32[]{:T(128)} %constant.36.clone.1, f32[512,256]{1,0:T(8,128)} %convolution_add_fusion, f32[512,256]{1,0:T(8,128)S(1)} %copy-done.2, f32[]{:T(128)} %constant.48.clone.1, pred[512]{0:T(512)(128)(4,1)S(1)} %get-tuple-element.10), kind=kCustom, calls=%fused_computation.17 | custom fusion | flops 393216 | bytes 2359816 | tf_op jit(solution)/shard_map/scatter-add | solution.py:56
  77.8 1.0 copy-done.4
  78.8 3.6 %scatter_custom_fusion.1 = f32[512,256]{1,0:T(8,128)S(1)} fusion(s32[512]{0:T(512)S(1)} %compare_select_fusion.5, f32[512,256]{1,0:T(8,128)S(1)} %copy-done.4, f32[512,256]{1,0:T(8,128)S(1)} %gather_fusion, f32[]{:T(128)} %constant.48.clone.1, f32[]{:T(128)} %constant.36.clone.1, pred[512]{0:T(512)(128)(4,1)S(1)} %get-tuple-element.11), kind=kCustom, calls=%fused_computation.24 | custom fusion | flops 393216 | bytes 1573384 | tf_op jit(solution)/shard_map/scatter-add | solution.py:64
  82.4 3.2 %fusion.36 = f32[512,256]{1,0:T(8,128)S(1)} fusion(f32[512,512]{1,0:T(8,128)} %copy-done.6, f32[512,256]{1,0:T(8,128)} %copy-done.5), kind=kOutput, calls=%fused_computation.77 | convolution fusion | flops 805306368 | bytes 2097152 | tf_op jit(solution)/shard_map/dot_general | solution.py:42
  85.5 3.8 %scatter_fusion = f32[512,256]{1,0:T(8,128)S(1)} fusion(f32[512,256]{1,0:T(8,128)S(1)} %scatter_custom_fusion.1, s32[512]{0:T(512)S(1)} %compare_select_fusion.3, f32[512,256]{1,0:T(8,128)S(1)} %fusion.36), kind=kCustom, calls=%fused_computation.7 | custom fusion | flops 131072 | bytes 1574912 | tf_op jit(solution)/shard_map/scatter-add | solution.py:66
  89.3 6.8 %scatter_fusion.1 = f32[512,256]{1,0:T(8,128)S(1)} fusion(f32[512,256]{1,0:T(8,128)S(1)} %scatter_fusion, s32[768]{0:T(1024)S(1)} %fusion.29, f32[768,256]{1,0:T(8,128)} %bitcast.11), kind=kCustom, calls=%fused_computation.9 | custom fusion | flops 196608 | bytes 2362368 | tf_op jit(solution)/shard_map/scatter-add | solution.py:68
  96.9 0.9 divide_subtract_fusion
  97.8 39.7 %reduce-scatter.2.cloned.1.call-done = f32[80,256]{1,0:T(8,128)} async-done(((f32[1280,256]{1,0:T(8,128)}), f32[80,256]{1,0:T(8,128)}) %reduce-scatter.2.cloned.1.call-update) | async-done | bytes 81936 | tf_op jit(solution)/shard_map/reduce_scatter | solution.py:58
  (45 shorter events, 2.0 us)
Async XLA Ops:
  7.2 33.1 %copy-start = (f32[1280,256]{1,0:T(8,128)S(1)}, f32[1280,256]{1,0:T(8,128)}, u32[]{:S(2)}) copy-start(f32[1280,256]{1,0:T(8,128)} %param.19) | copy-start | bytes 3932164
  14.1 11.8 %all-to-all-start = ((s32[8,96,1]{1,2,0:T(1,128)}), s32[8,96,1]{1,2,0:T(1,128)S(1)}, u32[]{:S(2)}, u32[]{:S(2)}) async-start(s32[8,96,1]{1,2,0:T(1,128)} %all_to_all.24), calls=%async_computation | async-start | bytes 8192 | tf_op jit(solution)/shard_map/all_to_all | solution.py:29
  30.4 4.6 %copy-start.1 = (f32[512,256]{1,0:T(8,128)S(1)}, f32[512,256]{1,0:T(8,128)}, u32[]{:S(2)}) copy-start(f32[512,256]{1,0:T(8,128)} %param.11) | copy-start | bytes 1572868
  31.5 24.4 %all-to-all-start.1 = ((f32[8,96,256]{2,1,0:T(8,128)}), f32[8,96,256]{2,1,0:T(8,128)S(1)}, u32[]{:S(2)}, u32[]{:S(2)}) async-start(f32[8,96,256]{2,1,0:T(8,128)} %broadcast_select_fusion), calls=%async_computation.1 | async-start | bytes 1572864 | tf_op jit(solution)/shard_map/all_to_all | solution.py:31
  35.0 2.3 %copy-start.8 = (s32[512]{0:T(512)S(1)}, s32[512]{0:T(512)}, u32[]{:S(2)}) copy-start(s32[512]{0:T(512)} %param.17) | copy-start | bytes 6148
  37.3 2.9 %copy-start.10 = (s32[512]{0:T(512)S(1)}, s32[512]{0:T(512)}, u32[]{:S(2)}) copy-start(s32[512]{0:T(512)} %param.16) | copy-start | bytes 6148
  40.3 1.6 %copy-start.9 = (s32[512]{0:T(512)S(1)}, s32[512]{0:T(512)}, u32[]{:S(2)}) copy-start(s32[512]{0:T(512)} %param.13) | copy-start | bytes 6148
  59.7 7.8 %copy-start.5 = (f32[512,256]{1,0:T(8,128)}, f32[512,256]{1,0:T(8,128)S(1)}, u32[]{:S(2)}) copy-start(f32[512,256]{1,0:T(8,128)S(1)} %get-tuple-element.7) | copy-start | bytes 1572868
  63.0 26.3 %all-to-all-start.2 = ((f32[8,96,256]{2,1,0:T(8,128)}), f32[8,96,256]{2,1,0:T(8,128)}, u32[]{:S(2)}, u32[]{:S(2)}) async-start(f32[8,96,256]{2,1,0:T(8,128)} %bitcast.26), calls=%async_computation.2 | async-start | bytes 1572864 | tf_op jit(solution)/shard_map/all_to_all | solution.py:57
  67.2 3.7 %copy-start.3 = (f32[512,256]{1,0:T(8,128)S(1)}, f32[512,256]{1,0:T(8,128)}, u32[]{:S(2)}) copy-start(f32[512,256]{1,0:T(8,128)} %gather_fusion.2) | copy-start | bytes 1572868
  67.2 70.3 %reduce-scatter.2.cloned.1.call-start = ((), (), s32[]{:S(2)}) async-start(), calls=%async_computation.4 | async-start | bytes 1392640 | tf_op jit(solution)/shard_map/reduce_scatter | solution.py:58
  67.5 3.4 %copy-start.7 = (f32[512,256]{1,0:T(8,128)S(1)}, f32[512,256]{1,0:T(8,128)}, u32[]{:S(2)}) copy-start(f32[512,256]{1,0:T(8,128)} %gather_fusion.4) | copy-start | bytes 1572868
  69.9 1.0 copy-start.6
  70.9 1.9 %copy-start.2 = (f32[512,256]{1,0:T(8,128)S(1)}, f32[512,256]{1,0:T(8,128)}, u32[]{:S(2)}) copy-start(f32[512,256]{1,0:T(8,128)} %gather_fusion.3) | copy-start | bytes 1572868
  77.8 1.0 copy-start.4
  89.3 6.9 %copy-start.11 = (f32[512]{0:T(512)S(1)}, f32[512]{0:T(512)}, u32[]{:S(2)}) copy-start(f32[512]{0:T(512)} %param.12) | copy-start | bytes 6148
Sparse Core Ops, SparseCore 0:
  77.9 59.5 reduce-scatter.1
where the time goes:
time: 145 us; the launch traced here: 144 us
  waiting for transfers between devices  58.5 us (40%)
  other arithmetic  31.5 us (22%)
  local copies, waits for them, and re-layouts  17.6 us (12%)
  between operations  15 us (10%)
  starting transfers between devices  14.3 us (10%)
  matrix products  7.42 us (5%)
    reduce_scatter x1, waiting for transfers between devices, body(): lax.psum_scatter(rel_part, ('owner', 'rep', 'sub'), scatter_dimension=0,...  39.7 us
    scatter-add x3, other arithmetic, body(): grad_rows = grad_rows.at[src_local].add(grad_source).at[neg_local].add(gr...  14.1 us
    all_to_all x1, waiting for transfers between devices, body(): lax.all_to_all(served, 'owner', split_axis=0, concat_axis=0, tiled=True)  14 us
    all_to_all x1, starting transfers between devices, body(): lax.all_to_all(wanted, 'owner', split_axis=0, concat_axis=0, tiled=True)  6.33 us
    scatter-add x1, other arithmetic, body(): jnp.zeros(relations.shape, jnp.float32).at[rel_ids].add(grad_operator)  5.02 us
    all_to_all x1, waiting for transfers between devices, body(): lax.all_to_all(wanted, 'owner', split_axis=0, concat_axis=0, tiled=True)  4.8 us
    all_to_all x1, starting transfers between devices, body(): lax.all_to_all(outgoing, 'owner', split_axis=0, concat_axis=0, tiled=True)  4.21 us
    all_to_all x1, starting transfers between devices, body(): lax.all_to_all(served, 'owner', split_axis=0, concat_axis=0, tiled=True)  3.55 us
  transfers between devices with their start and end apart: 4, of which 3 were waited for; matrix products, arithmetic and copies ran while one was open for 24% of the time, Pallas kernels for 0%

commit v1 on v0

v1 whole, which is shorter than its diff:
```python
import functools

import jax
import jax.numpy as jnp
from jax import lax
from jax.experimental import pallas as pl
from jax.experimental.pallas import tpu as pltpu
from jax.sharding import PartitionSpec as P

step_size = 0.1
F32 = jnp.float32
BF16 = jnp.bfloat16
MESH = pl.DeviceIdType.MESH


def iota(shape, dim):
    return lax.broadcasted_iota(jnp.int32, shape, dim).astype(F32)


def dot(a, b):
    return lax.dot_general(a, b, (((1,), (0,)), ((), ())), preferred_element_type=F32)


def dot_nt(a, b):
    return lax.dot_general(a, b, (((1,), (1,)), ((), ())), preferred_element_type=F32)


def split(x):
    hi = x.astype(BF16)
    return hi, (x - hi.astype(F32)).astype(BF16)


def put_split(ref, rows, x):
    width = x.shape[1]
    hi, lo = split(x)
    ref[rows, 0:width] = hi
    ref[rows, width:] = lo


def fold(x):
    width = x.shape[1] // 2
    return x[:, :width] + x[:, width:]


def onehot(a, b):
    return jnp.where(a == b, 1.0, 0.0).astype(BF16)


def each(count, step):
    if count <= 8:
        for k in range(count):
            step(k)
    else:

        @pl.loop(0, count)
        def _(k):
            step(k)


def kernel(
    dims,
    ent,
    ada,
    src,
    dpart,
    dloc,
    rel,
    neg,
    cnt,
    relations,
    rows_out,
    ada_out,
    rel_out,
    ids_out,
    ids_in,
    ent_hl,
    rel_hl,
    neg_hl,
    served,
    fetched,
    outgoing,
    incoming,
    q_s,
    source_s,
    oper_s,
    gq_s,
    q_hl,
    go_hl,
    act_s,
    frow,
    gneg,
    rel_part,
    recv1,
    recv2,
    recv3,
    ids_send,
    ids_recv,
    row_send,
    row_recv,
    grad_send,
    grad_recv,
    s1_send,
    s1_recv,
    s2_send,
    s2_recv,
    s3_send,
    s3_recv,
):
    n, reps, subs, cores, zs, cap, shard, pad = dims
    me = lax.axis_index("owner")
    x = lax.axis_index("rep")
    edges = src.shape[1]
    rows, width = ent.shape
    slots = n * cap
    rels = relations.shape[0]
    chunk = 256 if slots % 256 == 0 else slots
    if subs > 1:
        c, z = lax.axis_index("sub"), me
    else:
        c, z = lax.rem(me, cores), lax.div(me, cores)

    def owner_peer(k):
        return lax.rem(me + k, n)

    def core_peer(k):
        p = lax.rem(c + k, cores)
        return p, ({"sub": p} if subs > 1 else {"owner": z * cores + p})

    def rep_peer(k):
        p = lax.rem(x + k, reps)
        return p, {"rep": p}

    def z_peer(k):
        p = lax.rem(z + k, zs)
        return p, ({"owner": p} if subs > 1 else {"owner": p * cores + c})

    barrier = pltpu.get_barrier_semaphore()

    def greet(device):
        pl.semaphore_signal(barrier, inc=1, device_id=device, device_id_type=MESH)

    each(n - 1, lambda k: greet({"owner": owner_peer(k + 1)}))
    each(reps - 1, lambda k: greet(rep_peer(k + 1)[1]))
    greeted = n - 1 + reps - 1
    if subs > 1:
        each(subs - 1, lambda k: greet(core_peer(k + 1)[1]))
        greeted += subs - 1

    def copy(source, target, send, recv, device):
        return pltpu.make_async_remote_copy(
            src_ref=source,
            dst_ref=target,
            send_sem=send,
            recv_sem=recv,
            device_id=device,
            device_id_type=MESH,
        )

    def ids_copy(p, s):
        return copy(ids_out.at[p], ids_in.at[s], ids_send.at[p], ids_recv.at[s], {"owner": p})

    def row_copy(p, s):
        return copy(served.at[p], fetched.at[s], row_send.at[p], row_recv.at[s], {"owner": p})

    def grad_copy(p, s):
        return copy(outgoing.at[p], incoming.at[s], grad_send.at[p], grad_recv.at[s], {"owner": p})

    dpart_row = dpart[...].astype(F32)
    pt = iota((n, edges), 0) == dpart_row
    before = dot(
        jnp.where(pt, 1.0, 0.0).astype(BF16),
        jnp.where(iota((edges, edges), 0) < iota((edges, edges), 1), 1.0, 0.0).astype(BF16),
    )
    rank = jnp.sum(jnp.where(pt, before, 0.0), axis=0, keepdims=True)
    slot_row = dpart_row * cap + rank

    def low_high(ref):
        v = ref[...]
        return (v & 255).astype(F32), (v >> 8).astype(F32)

    rt = onehot(iota((128, edges), 0), rank)
    low, high = low_high(dloc)
    wanted = dot_nt(jnp.where(pt, low, 0.0).astype(BF16), rt) + 256.0 * dot_nt(
        jnp.where(pt, high, 0.0).astype(BF16), rt
    )
    for p in range(n):
        ids_out[p] = wanted[p : p + 1, :]
    pl.semaphore_wait(barrier, greeted)
    each(n - 1, lambda k: ids_copy(owner_peer(k + 1), me).start())
    ids_in[me] = ids_out[me]

    put_split(ent_hl, pl.ds(0, rows), ent[...])

    def id_column(s):
        return jnp.transpose(jnp.broadcast_to(ids_in[s], (8, 128)))[:cap, 0:1]

    def serve(s):
        return fold(dot(onehot(id_column(s), iota((cap, rows), 1)), ent_hl[...]))

    def serve_peer(k):
        p = owner_peer(k + 1)
        ids_copy(p, p).wait_recv()
        served[p] = serve(p)
        row_copy(p, me).start()

    each(n - 1, serve_peer)
    fetched[me] = serve(me)

    src_low, src_high = low_high(src)
    rel_low, rel_high = low_high(rel)
    active = jnp.where(
        lax.broadcasted_iota(jnp.int32, (1, edges), 1) < cnt[...], 1.0, 0.0
    )
    fields = jnp.concatenate(
        [src_low, src_high, rel_low, rel_high, active, jnp.zeros((11, edges), F32)], axis=0
    ).astype(BF16)
    for t in range(rels // 256):
        put_split(rel_hl, pl.ds(t * 256, 256), relations[pl.ds(t * 256, 256), :])
    neg_col = jnp.transpose(jnp.broadcast_to(neg[...].astype(F32), (8, edges)))[:, 0:1]
    neg_hl[...] = dot(onehot(neg_col, iota((edges, rows), 1)), ent_hl[...]).astype(BF16)
    gneg[...] = jnp.zeros_like(gneg)

    @pl.loop(0, slots // chunk)
    def _(t):
        at = pl.ds(pl.multiple_of(t * chunk, chunk), chunk)
        first = (t * chunk).astype(F32)
        st = onehot(iota((chunk, edges), 0) + first, slot_row)
        fcol = dot_nt(st, fields)
        frow[:, at] = dot_nt(fields, st)
        src_col = fcol[:, 0:1] + 256.0 * fcol[:, 1:2]
        rel_col = fcol[:, 2:3] + 256.0 * fcol[:, 3:4]
        act_col = fcol[:, 4:5]
        act_s[at, :] = act_col
        source = fold(dot(onehot(src_col, iota((chunk, rows), 1)), ent_hl[...]))
        operator = fold(dot(onehot(rel_col, iota((chunk, rels), 1)), rel_hl[...]))
        queries = source * operator
        source_s[at, :] = source
        oper_s[at, :] = operator
        q_s[at, :] = queries
        q_hi, q_lo = split(queries)
        q_hl[:, :width] = q_hi
        q_hl[:, width:] = q_lo
        n_hi = neg_hl[:, :width]
        n_lo = neg_hl[:, width:]
        scores = dot_nt(q_hi, n_hi) + (dot_nt(q_hi, n_lo) + dot_nt(q_lo, n_hi))
        gn = jax.nn.sigmoid(scores) * (act_col / edges_neg(neg))
        gn_hi, gn_lo = split(gn)
        gq_s[at, :] = fold(dot(gn_hi, neg_hl[...])) + dot(gn_lo, n_hi)
        gt_hi, gt_lo = split(jnp.transpose(gn))
        gneg[...] += fold(dot(gt_hi, q_hl[...])) + dot(gt_lo, q_hi)

    def block_rows(p):
        return pl.ds(pl.multiple_of(p * cap, 8), cap)

    def score(p, out):
        at = block_rows(p)
        target = fetched[p]
        queries = q_s[at, :]
        positive = jnp.sum(queries * target, axis=1, keepdims=True)
        grad_pos = -jax.nn.sigmoid(-positive) * act_s[at, :]
        out[...] = grad_pos * queries
        gq_s[at, :] += grad_pos * target

    score(me, incoming.at[me])

    def score_peer(k):
        p = owner_peer(n - 1 - k)
        row_copy(p, p).wait_recv()
        score(p, outgoing.at[p])
        grad_copy(p, me).start()

    each(n - 1, score_peer)

    for t in range(slots // chunk):
        at = pl.ds(t * chunk, chunk)
        put_split(go_hl, at, gq_s[at, :] * source_s[at, :])
    rel_row = frow[2:3, :] + 256.0 * frow[3:4, :]
    block = zs * pad

    def rel_block(cc, xx):
        local = iota((block, 1), 0)
        zz = jnp.floor((local + 0.5) * (1.0 / pad))
        within = local - zz * pad
        cf, xf = cc.astype(F32), xx.astype(F32)
        if subs > 1:
            dev = (zz * reps + xf) * subs + cf
        else:
            dev = (zz * cores + cf) * reps + xf
        ident = jnp.where(within < shard, dev * shard + within, -1.0)
        rel_part[cc, xx] = fold(dot(onehot(ident, rel_row), go_hl[...]))

    def s1_copy(p, device, s):
        return copy(rel_part.at[p], recv1.at[s], s1_send.at[p], s1_recv.at[s], device)

    def s2_copy(p, device, s):
        return copy(rel_part.at[c, p], recv2.at[s], s2_send.at[p], s2_recv.at[s], device)

    def s3_copy(p, device, s):
        return copy(
            rel_part.at[c, x, pl.ds(pl.multiple_of(p * pad, 8), pad)],
            recv3.at[s],
            s3_send.at[p],
            s3_recv.at[s],
            device,
        )

    def s1_start(k):
        p, device = core_peer(k + 1)
        for r in range(reps):
            rel_block(p, rep_peer(r)[0])
        s1_copy(p, device, c).start()

    each(cores - 1, s1_start)
    for r in range(reps):
        rel_block(c, rep_peer(r)[0])

    def s1_wait(k):
        p, device = core_peer(k + 1)
        s1_copy(p, device, p).wait_recv()
        for r in range(reps):
            rel_part[c, r] += recv1[p, r]

    each(cores - 1, s1_wait)

    def s2_start(k):
        p, device = rep_peer(k + 1)
        s2_copy(p, device, x).start()

    each(reps - 1, s2_start)

    src_row = frow[0:1, :] + 256.0 * frow[1:2, :]
    for t in range(slots // chunk):
        at = pl.ds(t * chunk, chunk)
        put_split(go_hl, at, gq_s[at, :] * oper_s[at, :])
    grad = fold(dot(onehot(iota((rows, slots), 0), src_row), go_hl[...]))
    gneg_hi, gneg_lo = split(gneg[...])
    neg_to = onehot(iota((rows, edges), 0), neg[...].astype(F32))
    gneg[...] = grad + (dot(neg_to, gneg_hi) + dot(neg_to, gneg_lo))

    def s2_wait(k):
        p, device = rep_peer(k + 1)
        s2_copy(p, device, p).wait_recv()
        rel_part[c, x] += recv2[p]

    each(reps - 1, s2_wait)

    def s3_start(k):
        p, device = z_peer(k + 1)
        s3_copy(p, device, z).start()

    each(zs - 1, s3_start)

    def gather_in(p):
        to = onehot(iota((rows, cap), 0), ids_in[p][:, :cap])
        hi, lo = split(incoming[p])
        gneg[...] += dot(to, hi) + dot(to, lo)

    gather_in(me)

    def gather_peer(k):
        p = owner_peer(k + 1)
        grad_copy(p, p).wait_recv()
        gather_in(p)

    each(n - 1, gather_peer)

    total = gneg[...]
    ada_col = jnp.transpose(jnp.broadcast_to(ada[...], (8, rows)))[:, 0:1]
    ada_new = ada_col + jnp.sum(total * total, axis=1, keepdims=True) * (1.0 / width)
    rows_out[...] = ent[...] - step_size * total / jnp.sqrt(ada_new)
    ada_out[...] = jnp.transpose(jnp.broadcast_to(ada_new, (rows, 128)))[0:1, :]

    rel_out[...] = rel_part[c, x, pl.ds(pl.multiple_of(z * pad, 8), pad)][:shard]

    def s3_wait(k):
        p, device = z_peer(k + 1)
        s3_copy(p, device, p).wait_recv()
        rel_out[...] += recv3[p][:shard]

    each(zs - 1, s3_wait)

    def drain(k):
        p = owner_peer(k + 1)
        ids_copy(p, me).wait_send()
        row_copy(p, me).wait_send()
        grad_copy(p, me).wait_send()

    each(n - 1, drain)

    def drain1(k):
        p, device = core_peer(k + 1)
        s1_copy(p, device, c).wait_send()

    def drain2(k):
        p, device = rep_peer(k + 1)
        s2_copy(p, device, x).wait_send()

    def drain3(k):
        p, device = z_peer(k + 1)
        s3_copy(p, device, z).wait_send()

    each(cores - 1, drain1)
    each(reps - 1, drain2)
    each(zs - 1, drain3)


def edges_neg(neg):
    return float(neg.shape[1])


def body(
    entity_rows,
    adagrad_sum,
    src_local,
    dst_part,
    dst_local,
    rel_ids,
    neg_local,
    edge_count,
    relations,
):
    n = lax.axis_size("owner")
    reps = lax.axis_size("rep")
    subs = lax.axis_size("sub")
    edges = src_local.shape[0]
    rows, width = entity_rows.shape
    rels = relations.shape[0]
    cap = edges // n * 3 // 2
    shard = rels // (n * reps * subs)
    pad = -(-shard // 8) * 8
    cores = subs if subs > 1 else (2 if n % 2 == 0 else 1)
    zs = n if subs > 1 else n // cores
    dims = (n, reps, subs, cores, zs, cap, shard, pad)
    slots = n * cap
    chunk = 256 if slots % 256 == 0 else slots
    vmem = pl.BlockSpec(memory_space=pltpu.VMEM)
    dma = pltpu.SemaphoreType.DMA

    def row(a):
        return a.reshape(1, -1)

    rows_new, ada_new, rel_grad = pl.pallas_call(
        functools.partial(kernel, dims),
        out_shape=(
            jax.ShapeDtypeStruct((rows, width), F32),
            jax.ShapeDtypeStruct((1, rows), F32),
            jax.ShapeDtypeStruct((shard, width), F32),
        ),
        in_specs=[vmem] * 9,
        out_specs=(vmem, vmem, vmem),
        scratch_shapes=[
            pltpu.VMEM((n, 1, 128), F32),
            pltpu.VMEM((n, 1, 128), F32),
            pltpu.VMEM((rows, 2 * width), BF16),
            pltpu.VMEM((rels, 2 * width), BF16),
            pltpu.VMEM((edges, 2 * width), BF16),
            pltpu.VMEM((n, cap, width), F32),
            pltpu.VMEM((n, cap, width), F32),
            pltpu.VMEM((n, cap, width), F32),
            pltpu.VMEM((n, cap, width), F32),
            pltpu.VMEM((slots, width), F32),
            pltpu.VMEM((slots, width), F32),
            pltpu.VMEM((slots, width), F32),
            pltpu.VMEM((slots, width), F32),
            pltpu.VMEM((chunk, 2 * width), BF16),
            pltpu.VMEM((slots, 2 * width), BF16),
            pltpu.VMEM((slots, 1), F32),
            pltpu.VMEM((16, slots), F32),
            pltpu.VMEM((rows, width), F32),
            pltpu.VMEM((cores, reps, zs * pad, width), F32),
            pltpu.VMEM((cores, reps, zs * pad, width), F32),
            pltpu.VMEM((reps, zs * pad, width), F32),
            pltpu.VMEM((zs, pad, width), F32),
            dma((n,)),
            dma((n,)),
            dma((n,)),
            dma((n,)),
            dma((n,)),
            dma((n,)),
            dma((cores,)),
            dma((cores,)),
            dma((reps,)),
            dma((reps,)),
            dma((zs,)),
            dma((zs,)),
        ],
        compiler_params=pltpu.CompilerParams(
            collective_id=0, has_side_effects=True, vmem_limit_bytes=48 * 1024 * 1024
        ),
        cost_estimate=pl.CostEstimate(
            flops=10_000_000_000, bytes_accessed=3_000_000, transcendentals=400_000
        ),
    )(
        entity_rows,
        row(adagrad_sum),
        row(src_local),
        row(dst_part),
        row(dst_local),
        row(rel_ids),
        row(neg_local),
        row(edge_count),
        relations,
    )
    return rows_new, ada_new.reshape(-1), rel_grad


def solution(mesh):
    split_rows = P(("parts", "owner", "rep", "sub"))
    split_wide = P(("parts", "owner", "rep", "sub"), None)
    in_specs = (
        split_wide,
        split_rows,
        split_rows,
        split_wide,
        split_rows,
        split_rows,
        split_rows,
        split_rows,
        P(),
    )
    out_specs = (split_wide, split_rows, split_wide)
    return jax.shard_map(body, mesh=mesh, in_specs=in_specs, out_specs=out_specs, check_vma=False)
```

time: 145 us -> 61.7 us (0.43)
  waiting for transfers between devices: 58.5 us -> 0 us
  Pallas kernels: 0 us -> 51.6 us
  other arithmetic: 31.5 us -> 0 us
  starting transfers between devices: 14.3 us -> 0 us
  between operations: 15 us -> 1.3 us
  local copies, waits for them, and re-layouts: 17.6 us -> 8.45 us
  matrix products: 7.42 us -> 0 us
    pallas_call x0 -> x1, Pallas kernels: none -> 51.6 us  [body(): pl.pallas_call(functools.partial(kernel, dims), out_shape=(jax.ShapeDtype...]
    reduce_scatter x1 -> x0, waiting for transfers between devices: 39.7 us -> none  [body(): lax.psum_scatter(rel_part, ('owner', 'rep', 'sub'), scatter_dimension=0,...]
    scatter-add x4 -> x0, other arithmetic: 19.1 us -> none  [the longest x3 14.1 us: body(): grad_rows = grad_rows.at[src_local].add(grad_source).at[neg_local].add(gr...]
    all_to_all x3 -> x0, waiting for transfers between devices: 18.8 us -> none  [the longest x1 14 us: body(): lax.all_to_all(served, 'owner', split_axis=0, concat_axis=0, tiled=True)]
    all_to_all x3 -> x0, starting transfers between devices: 14.1 us -> none  [the longest x1 6.33 us: body(): lax.all_to_all(wanted, 'owner', split_axis=0, concat_axis=0, tiled=True)]
    gather x5 -> x0, local copies, waits for them, and re-layouts: 11.4 us -> none  [the longest x1 3.15 us: body(): served = jnp.take(entity_rows, asked_ids, axis=0)]
    dot_general x3 -> x0, matrix products: 7.42 us -> none  [the longest x1 3.16 us: body(): jnp.dot(grad_neg.T, queries, precision=lax.Precision.HIGHEST, preferred_e...]
    unnamed x24 -> x19, local copies, waits for them, and re-layouts: 2.06 us -> 8.45 us
  transfers between devices with their start and end apart: 4 -> 0, of which waited for: 3 -> 0; matrix products, arithmetic and copies ran while one was open for 24% -> 0% of each run, Pallas kernels for 0% -> 0%
where the time goes in v1:
time: 61.7 us; the launch traced here: 61.4 us
  Pallas kernels  51.6 us (84%)
  local copies, waits for them, and re-layouts  8.45 us (14%)
  between operations  1.3 us (2%)
    pallas_call x1, Pallas kernels, body(): pl.pallas_call(functools.partial(kernel, dims), out_shape=(jax.ShapeDtype...  51.6 us
    unnamed x19, local copies, waits for them, and re-layouts  8.45 us

profile of v1, /device:TPU:0, one launch (start us, length us, event | category | flops | bytes accessed | tf_op | source)
XLA Modules:
  0.0 61.4 jit_solution(13803370086628677841)
XLA Ops:
  1.3 0.0 copy-start
  1.3 1.3 %copy-done = f32[1280,256]{1,0:T(8,128)S(1)} copy-done((f32[1280,256]{1,0:T(8,128)S(1)}, f32[1280,256]{1,0:T(8,128)}, u32[]{:S(2)}) %copy-start) | copy-done | bytes 1310744
  2.6 0.0 copy-start.1
  2.6 1.0 %copy-done.1 = f32[512,256]{1,0:T(8,128)S(1)} copy-done((f32[512,256]{1,0:T(8,128)S(1)}, f32[512,256]{1,0:T(8,128)}, u32[]{:S(2)}) %copy-start.1) | copy-done | bytes 524312
  3.6 0.0 copy-start.2
  3.6 0.7 %copy-done.2 = f32[512]{0:T(512)S(1)} copy-done((f32[512]{0:T(512)S(1)}, f32[512]{0:T(512)}, u32[]{:S(2)}) %copy-start.2) | copy-done | bytes 2072
  4.3 0.0 copy-start.3
  4.3 0.7 %copy-done.3 = s32[512]{0:T(512)S(1)} copy-done((s32[512]{0:T(512)S(1)}, s32[512]{0:T(512)}, u32[]{:S(2)}) %copy-start.3) | copy-done | bytes 2072
  5.0 0.0 copy-start.4
  5.0 0.7 %copy-done.4 = s32[512,1]{0,1:T(1,128)S(1)} copy-done((s32[512,1]{0,1:T(1,128)S(1)}, s32[512,1]{0,1:T(1,128)}, u32[]{:S(2)}) %copy-start.4) | copy-done | bytes 2072
  5.7 0.0 copy-start.5
  5.7 0.7 %copy-done.5 = s32[512]{0:T(512)S(1)} copy-done((s32[512]{0:T(512)S(1)}, s32[512]{0:T(512)}, u32[]{:S(2)}) %copy-start.5) | copy-done | bytes 2072
  6.4 0.0 copy-start.6
  6.4 0.7 %copy-done.6 = s32[512]{0:T(512)S(1)} copy-done((s32[512]{0:T(512)S(1)}, s32[512]{0:T(512)}, u32[]{:S(2)}) %copy-start.6) | copy-done | bytes 2072
  7.0 0.0 copy-start.7
  7.1 0.7 %copy-done.7 = s32[512]{0:T(512)S(1)} copy-done((s32[512]{0:T(512)S(1)}, s32[512]{0:T(512)}, u32[]{:S(2)}) %copy-start.7) | copy-done | bytes 2072
  7.7 51.6 %shard_map.112 = (f32[512,256]{1,0:T(8,128)S(1)}, f32[1,512]{1,0:T(1,128)S(1)}, f32[80,256]{1,0:T(8,128)S(1)}) custom-call(f32[512,256]{1,0:T(8,128)S(1)} %copy-done.1, f32[1,512]{1,0:T(1,128)S(1)} %bitcast.10, s32[1,512]{1,0:T(1,128)S(1)} %bitcast.11, s32[1,512]{1,0:T(1,128)S(1)} %bitcast.12, s32[1,512]{1,0:T(1,128)S(1)} %bitcast.13, ...), custom_call_target="tpu_custom_call" | custom-call | flops 10000000000 | bytes 3000000 | tf_op jit(solution)/shard_map/pallas_call | solution.py:442
  59.4 0.8 %copy.16 = f32[512,256]{1,0:T(8,128)} copy(f32[512,256]{1,0:T(8,128)S(1)} %get-tuple-element.12) | data formatting | bytes 1048576
  60.1 0.6 copy.17
  60.7 0.6 %copy.18 = f32[80,256]{1,0:T(8,128)} copy(f32[80,256]{1,0:T(8,128)S(1)} %get-tuple-element.14) | data formatting | bytes 163840
Async XLA Ops:
  1.3 1.3 %copy-start = (f32[1280,256]{1,0:T(8,128)S(1)}, f32[1280,256]{1,0:T(8,128)}, u32[]{:S(2)}) copy-start(f32[1280,256]{1,0:T(8,128)} %relations.1) | copy-start | bytes 3932164
  2.6 1.0 %copy-start.1 = (f32[512,256]{1,0:T(8,128)S(1)}, f32[512,256]{1,0:T(8,128)}, u32[]{:S(2)}) copy-start(f32[512,256]{1,0:T(8,128)} %ent.1) | copy-start | bytes 1572868
  3.6 0.7 %copy-start.2 = (f32[512]{0:T(512)S(1)}, f32[512]{0:T(512)}, u32[]{:S(2)}) copy-start(f32[512]{0:T(512)} %param.10) | copy-start | bytes 6148
  4.3 0.7 %copy-start.3 = (s32[512]{0:T(512)S(1)}, s32[512]{0:T(512)}, u32[]{:S(2)}) copy-start(s32[512]{0:T(512)} %param.11) | copy-start | bytes 6148
  5.0 0.7 %copy-start.4 = (s32[512,1]{0,1:T(1,128)S(1)}, s32[512,1]{0,1:T(1,128)}, u32[]{:S(2)}) copy-start(s32[512,1]{0,1:T(1,128)} %param.12) | copy-start | bytes 6148
  5.7 0.7 %copy-start.5 = (s32[512]{0:T(512)S(1)}, s32[512]{0:T(512)}, u32[]{:S(2)}) copy-start(s32[512]{0:T(512)} %param.13) | copy-start | bytes 6148
  6.4 0.7 %copy-start.6 = (s32[512]{0:T(512)S(1)}, s32[512]{0:T(512)}, u32[]{:S(2)}) copy-start(s32[512]{0:T(512)} %param.14) | copy-start | bytes 6148
  7.0 0.7 %copy-start.7 = (s32[512]{0:T(512)S(1)}, s32[512]{0:T(512)}, u32[]{:S(2)}) copy-start(s32[512]{0:T(512)} %param.15) | copy-start | bytes 6148

commit v2 on v1

--- a/solution.py
+++ b/solution.py
@@ -59,15 +59,15 @@
 
 def kernel(
     dims,
-    ent,
-    ada,
-    src,
-    dpart,
-    dloc,
-    rel,
-    neg,
+    ent_in,
+    ada_in,
+    src_in,
+    dpart_in,
+    dloc_in,
+    rel_in,
+    neg_in,
     cnt,
-    relations,
+    relations_in,
     rows_out,
     ada_out,
     rel_out,
@@ -105,8 +105,32 @@
     s2_recv,
     s3_send,
     s3_recv,
+    ent,
+    ada,
+    src,
+    dpart,
+    dloc,
+    rel,
+    neg,
+    relations,
+    load_sem,
 ):
     n, reps, subs, cores, zs, cap, shard, pad = dims
+    pairs = (
+        (dpart_in, dpart),
+        (dloc_in, dloc),
+        (ent_in, ent),
+        (src_in, src),
+        (rel_in, rel),
+        (neg_in, neg),
+        (relations_in, relations),
+        (ada_in, ada),
+    )
+    loads = [
+        pltpu.make_async_copy(a, b, load_sem.at[i]) for i, (a, b) in enumerate(pairs)
+    ]
+    for load in loads:
+        load.start()
     me = lax.axis_index("owner")
     x = lax.axis_index("rep")
     edges = src.shape[1]
@@ -165,6 +189,8 @@
     def grad_copy(p, s):
         return copy(outgoing.at[p], incoming.at[s], grad_send.at[p], grad_recv.at[s], {"owner": p})
 
+    loads[0].wait()
+    loads[1].wait()
     dpart_row = dpart[...].astype(F32)
     pt = iota((n, edges), 0) == dpart_row
     before = dot(
@@ -189,6 +215,7 @@
     each(n - 1, lambda k: ids_copy(owner_peer(k + 1), me).start())
     ids_in[me] = ids_out[me]
 
+    loads[2].wait()
     put_split(ent_hl, pl.ds(0, rows), ent[...])
 
     def id_column(s):
@@ -206,6 +233,8 @@
     each(n - 1, serve_peer)
     fetched[me] = serve(me)
 
+    for load in loads[3:]:
+        load.wait()
     src_low, src_high = low_high(src)
     rel_low, rel_high = low_high(rel)
     active = jnp.where(
@@ -434,6 +463,8 @@
     slots = n * cap
     chunk = 256 if slots % 256 == 0 else slots
     vmem = pl.BlockSpec(memory_space=pltpu.VMEM)
+    hbm = pl.BlockSpec(memory_space=pltpu.HBM)
+    ids_row = pltpu.VMEM((1, edges), jnp.int32)
     dma = pltpu.SemaphoreType.DMA
 
     def row(a):
@@ -446,7 +477,7 @@
             jax.ShapeDtypeStruct((1, rows), F32),
             jax.ShapeDtypeStruct((shard, width), F32),
         ),
-        in_specs=[vmem] * 9,
+        in_specs=[hbm] * 7 + [vmem, hbm],
         out_specs=(vmem, vmem, vmem),
         scratch_shapes=[
             pltpu.VMEM((n, 1, 128), F32),
@@ -483,9 +514,18 @@
             dma((reps,)),
             dma((zs,)),
             dma((zs,)),
+            pltpu.VMEM((rows, width), F32),
+            pltpu.VMEM((1, rows), F32),
+            ids_row,
+            ids_row,
+            ids_row,
+            ids_row,
+            ids_row,
+            pltpu.VMEM((rels, width), F32),
+            dma((8,)),
         ],
         compiler_params=pltpu.CompilerParams(
-            collective_id=0, has_side_effects=True, vmem_limit_bytes=48 * 1024 * 1024
+            collective_id=0, has_side_effects=True, vmem_limit_bytes=62 * 1024 * 1024
         ),
         cost_estimate=pl.CostEstimate(
             flops=10_000_000_000, bytes_accessed=3_000_000, transcendentals=400_000

time: 61.7 us -> 58.8 us (0.953)
  local copies, waits for them, and re-layouts: 8.45 us -> 4.64 us
  Pallas kernels: 51.6 us -> 52.6 us
    unnamed x19 -> x3, local copies, waits for them, and re-layouts: 8.45 us -> 4.64 us
    pallas_call x1, Pallas kernels: 51.6 us -> 52.6 us  [body(): pl.pallas_call(functools.partial(kernel, dims), out_shape=(jax.ShapeDtype...]
where the time goes in v2:
time: 58.8 us; the launch traced here: 58.6 us
  Pallas kernels  52.6 us (89%)
  local copies, waits for them, and re-layouts  4.64 us (8%)
  between operations  1.29 us (2%)
    pallas_call x1, Pallas kernels, body(): pl.pallas_call(functools.partial(kernel, dims), out_shape=(jax.ShapeDtype...  52.6 us
    unnamed x3, local copies, waits for them, and re-layouts  4.64 us

profile of v2, /device:TPU:0, one launch (start us, length us, event | category | flops | bytes accessed | tf_op | source)
XLA Modules:
  0.0 58.6 jit_solution(5654511876848414041)
XLA Ops:
  1.3 52.6 %shard_map.112 = (f32[512,256]{1,0:T(8,128)}, f32[1,512]{1,0:T(1,128)}, f32[80,256]{1,0:T(8,128)}) custom-call(f32[512,256]{1,0:T(8,128)} %ent_in.1, f32[1,512]{1,0:T(1,128)} %bitcast.10, s32[1,512]{1,0:T(1,128)} %bitcast.11, s32[1,512]{1,0:T(1,128)} %bitcast.12, s32[1,512]{1,0:T(1,128)} %bitcast.13, s32[1,512]{1,0:T(1,128)} %bitcast.14, s32[1,512]{1,0:T(1,128)} %bitcast.15, ...), custom_call_target="tpu_custom_call" | custom-call | flops 10000000000 | bytes 3000000 | tf_op jit(solution)/shard_map/pallas_call | solution.py:473
  53.9 1.9 %copy.16 = f32[512,256]{1,0:T(8,128)} copy(f32[512,256]{1,0:T(8,128)} %get-tuple-element.12) | data formatting | bytes 1048576
  55.8 1.2 %copy.17 = f32[512]{0:T(512)} copy(f32[512]{0:T(512)} %bitcast.9) | data formatting | bytes 4096
  57.0 1.5 %copy.18 = f32[80,256]{1,0:T(8,128)} copy(f32[80,256]{1,0:T(8,128)} %get-tuple-element.14) | data formatting | bytes 163840

commit v3 on v2

--- a/solution.py
+++ b/solution.py
@@ -144,7 +144,7 @@
         c, z = lax.rem(me, cores), lax.div(me, cores)
 
     def owner_peer(k):
-        return lax.rem(me + k, n)
+        return lax.rem(me + n // 2 + (k // 2 if k % 2 == 0 else -(k // 2)) + n, n) if n <= 8 else lax.rem(me + k, n)
 
     def core_peer(k):
         p = lax.rem(c + k, cores)

time: 58.8 us -> 58.3 us (level)
  no operation moved by 1% of the time
where the time goes in v3:
time: 58.3 us; the launch traced here: 58.1 us
  Pallas kernels  52.1 us (89%)
  local copies, waits for them, and re-layouts  4.64 us (8%)
  between operations  1.29 us (2%)
    pallas_call x1, Pallas kernels, body(): pl.pallas_call(functools.partial(kernel, dims), out_shape=(jax.ShapeDtype...  52.1 us
    unnamed x3, local copies, waits for them, and re-layouts  4.64 us

profile of v3, /device:TPU:0, one launch (start us, length us, event | category | flops | bytes accessed | tf_op | source)
XLA Modules:
  0.0 58.1 jit_solution(16864268069831265583)
XLA Ops:
  1.3 52.1 %shard_map.112 = (f32[512,256]{1,0:T(8,128)}, f32[1,512]{1,0:T(1,128)}, f32[80,256]{1,0:T(8,128)}) custom-call(f32[512,256]{1,0:T(8,128)} %ent_in.1, f32[1,512]{1,0:T(1,128)} %bitcast.10, s32[1,512]{1,0:T(1,128)} %bitcast.11, s32[1,512]{1,0:T(1,128)} %bitcast.12, s32[1,512]{1,0:T(1,128)} %bitcast.13, s32[1,512]{1,0:T(1,128)} %bitcast.14, s32[1,512]{1,0:T(1,128)} %bitcast.15, ...), custom_call_target="tpu_custom_call" | custom-call | flops 10000000000 | bytes 3000000 | tf_op jit(solution)/shard_map/pallas_call | solution.py:473
  53.4 1.9 %copy.16 = f32[512,256]{1,0:T(8,128)} copy(f32[512,256]{1,0:T(8,128)} %get-tuple-element.12) | data formatting | bytes 1048576
  55.3 1.2 %copy.17 = f32[512]{0:T(512)} copy(f32[512]{0:T(512)} %bitcast.9) | data formatting | bytes 4096
  56.5 1.5 %copy.18 = f32[80,256]{1,0:T(8,128)} copy(f32[80,256]{1,0:T(8,128)} %get-tuple-element.14) | data formatting | bytes 163840
